TPU v7x, 128 devices: a whole 4x4x4 slice. The times are simulated.
128 devices in a mesh: replica: 8 (over x_lo, y), fsdp: 16 (over x_hi, z, core).
Axes of the slice: x: 4 (x_hi: 2, x_lo: 2; x = x_hi * 2 + x_lo), y: 4, z: 4, core: 2. Of those that a mesh axis runs over, the one named last changes fastest.
Arguments:
- step_index: int32 [], replicated, may hold values from 1 to 63
- hidden: bfloat16 [8, 2, 1024, 6912], P('replica', None, 'fsdp'), may hold values from -6 to 6
- out_grad: bfloat16 [8, 2, 1024, 5120], P('replica', None, 'fsdp'), may hold values from -6 to 6
- weight: bfloat16 [8, 6912, 5120], P('replica', 'fsdp'), may hold values from -3 to 3
- moment: bfloat16 [8, 6912, 5120], P('replica', 'fsdp'), may hold values from -3 to 3
- second: bfloat16 [8, 6912, 5120], P('replica', 'fsdp'), may hold values from 0.0099487305 to 1
Outputs:
- new_weight: bfloat16 [8, 6912, 5120], P('replica', 'fsdp')
- new_moment: bfloat16 [8, 6912, 5120], P('replica', 'fsdp')
- hidden_grad: bfloat16 [8, 2, 1024, 6912], P('replica', None, 'fsdp')
Inputs may be any that keep to these rules, and one draw needn't show every extreme that they name: `step_index`: the step index of the update; it selects the distance of the averaging partner.
All inputs are finite; a program needn't handle non-finite values.
Results may differ from a plain program's by a relative error of at most 0.0052.
Values may be sent and summed in bfloat16 or wider, within the bound.
A program may use at most 128 MiB of HBM per device.

v0:
```python
from functools import partial

import jax
import jax.numpy as jnp
from jax import lax
from jax.sharding import PartitionSpec as P

beta_one = 0.9
beta_two = 0.95
learn_rate = 0.05
decay_rate = 0.4
epsilon = 1e-08


def shortened(array):

    def short(part):
        return part.astype(jnp.bfloat16) if part.dtype == jnp.float32 else part

    return jax.tree.map(short, array)


def shifted(block, axis, distance):
    devices = range(lax.axis_size(axis))
    route = [((i - distance) % len(devices), i) for i in devices]
    return lax.ppermute(block, axis, route)


def hidden_product(gathered, weight_rows, factor):
    product = factor * lax.dot_general(
        gathered, weight_rows, (((1,), (1,)), ((), ())), preferred_element_type=jnp.float32
    )
    return product.astype(jnp.bfloat16)


def gradient_rows(token_hidden, token_grads, factor):
    spread_rows = lax.all_to_all(token_hidden, "fsdp", split_axis=1, concat_axis=0, tiled=True)
    gathered = lax.all_gather(token_grads, "fsdp", axis=0, tiled=True)
    gradient = factor * lax.dot_general(
        spread_rows, gathered, (((0,), (0,)), ((), ())), preferred_element_type=jnp.float32
    )
    return (gradient, gathered, None)


def return_rows(gathered, hidden_part, weight_rows, factor):
    hidden_part = hidden_product(gathered, weight_rows, factor)
    return lax.all_to_all(hidden_part, "fsdp", split_axis=0, concat_axis=1, tiled=True)


def gossip_branch(stepped, distance):
    return jax.tree.map(
        lambda part, own: part.astype(own.dtype),
        shifted(shortened(stepped), "replica", distance),
        stepped,
    )


def adam_gossip(step_index, gradient, weight_rows, moment, second):
    step_float = step_index.astype(jnp.float32)
    first_moment = beta_one * moment[0].astype(jnp.float32) + (1.0 - beta_one) * gradient
    variance = beta_two * second[0].astype(jnp.float32) + (1.0 - beta_two) * gradient * gradient
    bias_one = 1.0 - beta_one**step_float
    bias_two = 1.0 - beta_two**step_float
    update = first_moment / bias_one / (jnp.sqrt(variance / bias_two) + epsilon)
    weight_wide = weight_rows.astype(jnp.float32)
    stepped = (weight_wide - learn_rate * (update + decay_rate * weight_wide)).astype(jnp.bfloat16)
    levels = lax.axis_size("replica").bit_length() - 1
    branches = [partial(gossip_branch, distance=1 << level_index) for level_index in range(levels)]
    partner = lax.switch(step_index % levels, branches, stepped)
    new_weight = (0.5 * (stepped.astype(jnp.float32) + partner.astype(jnp.float32))).astype(
        jnp.bfloat16
    )
    return (new_weight[None], first_moment.astype(jnp.bfloat16)[None])


def on_device(step_index, hidden, out_grad, weight, moment, second):
    weight_rows = weight[0]
    micro_count = hidden.shape[1]
    hidden_width = hidden.shape[3]
    factor = hidden_width ** (-0.5)
    groups = [
        (hidden[0, micro_index], out_grad[0, micro_index]) for micro_index in range(micro_count)
    ]
    gradient = None
    pending = []
    for token_hidden, token_grads in groups:
        part_grad, gathered, hidden_part = gradient_rows(token_hidden, token_grads, factor)
        gradient = part_grad if gradient is None else gradient + part_grad
        pending.append((gathered, hidden_part))
    pieces = [
        return_rows(gathered, hidden_part, weight_rows, factor) for gathered, hidden_part in pending
    ]
    new_weight, new_moment = adam_gossip(step_index, gradient, weight_rows, moment, second)
    hidden_grad = jnp.stack(pieces, 0).reshape(hidden.shape)
    return (new_weight, new_moment, hidden_grad)


def solution(mesh):
    placed = (
        P(),
        P("replica", None, "fsdp", None),
        P("replica", None, "fsdp", None),
        P("replica", "fsdp", None),
        P("replica", "fsdp", None),
        P("replica", "fsdp", None),
    )
    return jax.shard_map(
        on_device,
        mesh=mesh,
        in_specs=placed,
        out_specs=(
            P("replica", "fsdp", None),
            P("replica", "fsdp", None),
            P("replica", None, "fsdp", None),
        ),
        check_vma=False,
    )
```

profile of v0, /device:TPU:113, one launch (start us, length us, event | category | flops | bytes accessed | tf_op | source)
XLA Modules:
  0.0 362.6 jit_solution(10112900196351840113)
XLA Ops:
  7.2 0.0 all-gather.7.cloned.1.call-start
  7.2 2.4 fusion.33
  9.7 0.0 all-gather.7.cloned.1.call-update
  9.7 0.0 all-gather.5.cloned.1.call-start
  9.7 0.7 all-gather.5.cloned.1.call-update
  10.4 1.6 fusion.32
  12.0 2.3 all_to_all.56
  14.3 1.5 copy.16
  15.8 7.3 %all-to-all-start.1 = ((bf16[64,16,432]{2,0,1:T(8,128)(2,1)}), bf16[64,16,432]{2,0,1:T(8,128)(2,1)S(1)}, u32[]{:S(2)}, u32[]{:S(2)}) async-start(bf16[64,16,432]{2,0,1:T(8,128)(2,1)} %copy.16), calls=%async_computation.1 | async-start | bytes 2097152 | tf_op jit(solution)/shard_map/all_to_all | solution.py:37
  23.9 2.3 all_to_all.52
  26.1 1.5 copy.15
  27.7 72.6 %all-gather.7.cloned.1.call-done = bf16[1,1,1024,5120]{3,2,1,0:T(8,128)(2,1)} async-done(((bf16[1,1,64,5120]{3,2,1,0:T(8,128)(2,1)}), bf16[1,1,1024,5120]{3,2,1,0:T(8,128)(2,1)}) %all-gather.7.cloned.1.call-update) | async-done | bytes 10485776 | tf_op jit(solution)/shard_map/all_gather | solution.py:38
  100.3 10.0 %multiply_convert_fusion.1 = bf16[1024,432]{0,1:T(8,128)(2,1)S(1)} fusion(bf16[1,432,5120]{2,1,0:T(8,128)(2,1)} %param.12, bf16[1,1,1024,5120]{3,2,1,0:T(8,128)(2,1)} %all-gather.7.cloned.1.call-done), kind=kOutput, calls=%fused_computation.29 | convolution fusion | flops 4530733056 | bytes 15794176 | tf_op jit(solution)/shard_map/dot_general | solution.py:30
  110.3 1.3 copy.19
  111.6 0.0 all-to-all-done.1
  111.6 5.8 %all-to-all-start = ((bf16[64,16,432]{2,0,1:T(8,128)(2,1)}), bf16[64,16,432]{2,0,1:T(8,128)(2,1)S(1)}, u32[]{:S(2)}, u32[]{:S(2)}) async-start(bf16[64,16,432]{2,0,1:T(8,128)(2,1)} %copy.15), calls=%async_computation | async-start | bytes 2097152 | tf_op jit(solution)/shard_map/all_to_all | solution.py:37
  117.5 12.3 %fusion.2 = f32[432,5120]{1,0:T(8,128)} fusion(bf16[1024,432]{1,0:T(8,128)(2,1)S(1)} %bitcast.74, bf16[1,1,1024,5120]{3,2,1,0:T(8,128)(2,1)} %all-gather.7.cloned.1.call-done), kind=kOutput, calls=%fused_computation.4 | convolution fusion | flops 4529848320 | bytes 20217856 | tf_op jit(solution)/shard_map/dot_general | solution.py:39
  129.7 6.9 %all-to-all-done = bf16[64,16,432]{2,0,1:T(8,128)(2,1)S(1)} async-done(((bf16[64,16,432]{2,0,1:T(8,128)(2,1)}), bf16[64,16,432]{2,0,1:T(8,128)(2,1)S(1)}, u32[]{:S(2)}, u32[]{:S(2)}) %all-to-all-start) | async-done | bytes 884768 | tf_op jit(solution)/shard_map/all_to_all | solution.py:37
  136.6 7.2 %all-to-all-start.3 = ((bf16[16,64,432]{2,1,0:T(8,128)(2,1)}), bf16[16,64,432]{2,1,0:T(8,128)(2,1)S(1)}, u32[]{:S(2)}, u32[]{:S(2)}) async-start(bf16[16,64,432]{2,1,0:T(8,128)(2,1)} %bitcast.13), calls=%async_computation.3 | async-start | bytes 2097152 | tf_op jit(solution)/shard_map/all_to_all | solution.py:47
  143.9 55.0 %all-gather.5.cloned.1.call-done = bf16[1,1,1024,5120]{3,2,1,0:T(8,128)(2,1)} async-done(((bf16[1,1,64,5120]{3,2,1,0:T(8,128)(2,1)}), bf16[1,1,1024,5120]{3,2,1,0:T(8,128)(2,1)}) %all-gather.5.cloned.1.call-update) | async-done | bytes 10485776 | tf_op jit(solution)/shard_map/all_gather | solution.py:38
  198.9 20.7 %fusion.20 = (bf16[1,432,5120]{2,1,0:T(8,128)(2,1)}, bf16[432,5120]{1,0:T(8,128)(2,1)}) fusion(bf16[1,432,5120]{2,1,0:T(8,128)(2,1)} %param.13, f32[]{:T(128)S(6)} %sub.10, bf16[1,432,5120]{2,1,0:T(8,128)(2,1)} %param.14, f32[]{:T(128)S(6)} %sub.9, bf16[1,432,5120]{2,1,0:T(8,128)(2,1)} %param.12, f32[432,5120]{1,0:T(8,128)} %fusion.2, ...), kind=kOutput, calls=%fused_computation.24 | convolution fusion | flops 4578508800 | bytes 42336264 | tf_op jit(solution)/shard_map/dot_general | solution.py:39
  219.6 10.0 %multiply_convert_fusion.2 = bf16[1024,432]{0,1:T(8,128)(2,1)S(1)} fusion(bf16[1,432,5120]{2,1,0:T(8,128)(2,1)} %param.12, bf16[1,1,1024,5120]{3,2,1,0:T(8,128)(2,1)} %all-gather.5.cloned.1.call-done), kind=kOutput, calls=%fused_computation.30 | convolution fusion | flops 4530733056 | bytes 15794176 | tf_op jit(solution)/shard_map/dot_general | solution.py:30
  229.7 1.3 copy.17
  231.0 97.2 %conditional.4 = (bf16[432,5120]{1,0:T(8,128)(2,1)}) conditional(s32[]{:T(128)} %clamp.3, bf16[432,5120]{1,0:T(8,128)(2,1)} %get-tuple-element.17, bf16[432,5120]{1,0:T(8,128)(2,1)} %get-tuple-element.17, bf16[432,5120]{1,0:T(8,128)(2,1)} %get-tuple-element.17), branch_computations={%region_0.1_spmd, %region_1.2_spmd, %region_2.3_spmd} | conditional | bytes 17694768
  231.0 0.9 collective-permute-start
  231.9 96.3 %collective-permute-done = bf16[432,5120]{1,0:T(8,128)(2,1)} collective-permute-done((bf16[432,5120]{1,0:T(8,128)(2,1)}, bf16[432,5120]{1,0:T(8,128)(2,1)}, u32[]{:S(2)}, u32[]{:S(2)}) %collective-permute-start) | collective-permute-done | bytes 4423712 | tf_op jit(solution)/shard_map/cond/branch_0_fun/ppermute | solution.py:26
  328.1 0.0 all-to-all-done.3
  328.1 6.5 %all-to-all-start.2 = ((bf16[16,64,432]{2,1,0:T(8,128)(2,1)}), bf16[16,64,432]{2,1,0:T(8,128)(2,1)S(1)}, u32[]{:S(2)}, u32[]{:S(2)}) async-start(bf16[16,64,432]{2,1,0:T(8,128)(2,1)} %bitcast.11), calls=%async_computation.2 | async-start | bytes 2097152 | tf_op jit(solution)/shard_map/all_to_all | solution.py:47
  334.7 7.2 %fusion.21 = bf16[1,432,5120]{2,1,0:T(8,128)(2,1)} fusion(bf16[432,5120]{1,0:T(8,128)(2,1)} %get-tuple-element.22, bf16[432,5120]{1,0:T(8,128)(2,1)} %get-tuple-element.17), kind=kLoop, calls=%fused_computation.25 | loop fusion | flops 11059200 | bytes 13271040 | tf_op jit(solution)/shard_map/broadcast_in_dim | solution.py:73
  341.9 0.6 copy.20
  342.5 2.4 stack.10
  344.9 6.2 %all-to-all-done.2 = bf16[16,64,432]{2,1,0:T(8,128)(2,1)S(1)} async-done(((bf16[16,64,432]{2,1,0:T(8,128)(2,1)}), bf16[16,64,432]{2,1,0:T(8,128)(2,1)S(1)}, u32[]{:S(2)}, u32[]{:S(2)}) %all-to-all-start.2) | async-done | bytes 884768 | tf_op jit(solution)/shard_map/all_to_all | solution.py:47
  351.1 0.6 copy.18
  351.7 1.5 stack.9
  353.2 2.5 maximum_bitcast_fusion
Async XLA Ops:
  7.2 93.2 %all-gather.7.cloned.1.call-start = ((), (), s32[]{:S(2)}) async-start(), calls=%async_computation.5 | async-start | bytes 11141120 | tf_op jit(solution)/shard_map/all_gather | solution.py:38
  9.7 189.2 %all-gather.5.cloned.1.call-start = ((), (), s32[]{:S(2)}) async-start(), calls=%async_computation.4 | async-start | bytes 11141120 | tf_op jit(solution)/shard_map/all_gather | solution.py:38
  15.8 95.8 %all-to-all-start.1 = ((bf16[64,16,432]{2,0,1:T(8,128)(2,1)}), bf16[64,16,432]{2,0,1:T(8,128)(2,1)S(1)}, u32[]{:S(2)}, u32[]{:S(2)}) async-start(bf16[64,16,432]{2,0,1:T(8,128)(2,1)} %copy.16), calls=%async_computation.1 | async-start | bytes 2097152 | tf_op jit(solution)/shard_map/all_to_all | solution.py:37
  111.6 25.0 %all-to-all-start = ((bf16[64,16,432]{2,0,1:T(8,128)(2,1)}), bf16[64,16,432]{2,0,1:T(8,128)(2,1)S(1)}, u32[]{:S(2)}, u32[]{:S(2)}) async-start(bf16[64,16,432]{2,0,1:T(8,128)(2,1)} %copy.15), calls=%async_computation | async-start | bytes 2097152 | tf_op jit(solution)/shard_map/all_to_all | solution.py:37
  136.6 191.5 %all-to-all-start.3 = ((bf16[16,64,432]{2,1,0:T(8,128)(2,1)}), bf16[16,64,432]{2,1,0:T(8,128)(2,1)S(1)}, u32[]{:S(2)}, u32[]{:S(2)}) async-start(bf16[16,64,432]{2,1,0:T(8,128)(2,1)} %bitcast.13), calls=%async_computation.3 | async-start | bytes 2097152 | tf_op jit(solution)/shard_map/all_to_all | solution.py:47
  231.0 97.2 %collective-permute-start = (bf16[432,5120]{1,0:T(8,128)(2,1)}, bf16[432,5120]{1,0:T(8,128)(2,1)}, u32[]{:S(2)}, u32[]{:S(2)}) collective-permute-start(bf16[432,5120]{1,0:T(8,128)(2,1)} %param), channel_id=1, source_target_pairs={{112,0},{0,16},{16,32},{32,48},{48,64},{64,80},{80,96},{96,112},{1... | collective-permute-start | bytes 13271048 | tf_op jit(solution)/shard_map/cond/branch_0_fun/ppermute | solution.py:26
  328.1 23.0 %all-to-all-start.2 = ((bf16[16,64,432]{2,1,0:T(8,128)(2,1)}), bf16[16,64,432]{2,1,0:T(8,128)(2,1)S(1)}, u32[]{:S(2)}, u32[]{:S(2)}) async-start(bf16[16,64,432]{2,1,0:T(8,128)(2,1)} %bitcast.11), calls=%async_computation.2 | async-start | bytes 2097152 | tf_op jit(solution)/shard_map/all_to_all | solution.py:47
Sparse Core Ops, SparseCore 0:
  10.5 89.8 all-gather.6
  103.4 95.5 all-gather.4
where the time goes:
time: 368 us; the launch traced here: 363 us
  waiting for transfers between devices  238 us (65%)
  matrix products  53 us (14%)
  starting transfers between devices  27.9 us (8%)
  local copies, waits for them, and re-layouts  19.3 us (5%)
  between operations  14.8 us (4%)
  other arithmetic  9.76 us (3%)
    all_gather x2, waiting for transfers between devices, gradient_rows(): gathered = lax.all_gather(token_grads, 'fsdp', axis=0, tiled=True)  128 us
    ppermute x1, waiting for transfers between devices, shifted(): return lax.ppermute(block, axis, route)  96.3 us
    dot_general x2, matrix products, gradient_rows(): lax.dot_general(spread_rows, gathered, (((0,), (0,)), ((), ())), preferre...  33 us
    dot_general x2, matrix products, hidden_product(): lax.dot_general(gathered, weight_rows, (((1,), (1,)), ((), ())), preferre...  20 us
    all_to_all x2, starting transfers between devices, return_rows(): lax.all_to_all(hidden_part, 'fsdp', split_axis=0, concat_axis=1, tiled=True)  13.8 us
    all_to_all x2, starting transfers between devices, gradient_rows(): lax.all_to_all(token_hidden, 'fsdp', split_axis=1, concat_axis=0, tiled=T...  13.1 us
    all_to_all x4, local copies, waits for them, and re-layouts, gradient_rows(): lax.all_to_all(token_hidden, 'fsdp', split_axis=1, concat_axis=0, tiled=T...  7.63 us
  transfers between devices with their start and end apart: 7, of which 5 were waited for; matrix products, arithmetic and copies ran while one was open for 19% of the time, Pallas kernels for 0%

commit v1 on v0

v1 whole, which is shorter than its diff:
```python
import functools

import jax
import jax.numpy as jnp
from jax import lax
from jax.experimental import pallas as pl
from jax.experimental.pallas import tpu as pltpu
from jax.sharding import PartitionSpec as P

beta_one = 0.9
beta_two = 0.95
learn_rate = 0.05
decay_rate = 0.4
epsilon = 1e-08

MESH = pl.DeviceIdType.MESH
GROUP = 16
REPLICAS = 8
LANES = 128
CHUNK = 256

TO_X, TO_NEXT, TO_PREV, CORE_OWN, ON_NEXT, ON_PREV, CORE_PREV, CORE_NEXT, CORE_FAR = range(9)
COPIES = 9


def slot_of(index):
    x_hi, z, core = index // 8, (index // 2) % 4, index % 2
    return z * 4 + core * 2 + x_hi


def step_kernel(
    distance,
    factor,
    scale_ref,
    hidden_hbm,
    grads_hbm,
    weight_hbm,
    moment_hbm,
    second_hbm,
    new_weight_hbm,
    new_moment_hbm,
    hidden_grad_hbm,
    gathered,
    token_hidden,
    hidden_out,
    hidden_in,
    hidden_t,
    total,
    stepped,
    partner,
    cotangent_out,
    cotangent_in,
    weight_buf,
    moment_buf,
    second_buf,
    new_moment_buf,
    new_weight_buf,
    load_sem,
    own_sem,
    param_sem,
    moment_out_sem,
    weight_out_sem,
    gather_send,
    gather_recv,
    hidden_send,
    hidden_recv,
    back_send,
    back_recv,
    gossip_send,
    gossip_recv,
):
    chunks = gathered.shape[0]
    rows = weight_buf.shape[1]
    micro, tokens = token_hidden.shape[0], token_hidden.shape[1]
    width = token_hidden.shape[2]
    unit = micro * tokens
    blocks = width // LANES

    replica = lax.axis_index("replica")
    index = lax.axis_index("fsdp")
    x_hi, z, core = index // 8, (index // 2) % 4, index % 2
    z_next, z_prev, z_far = (z + 1) % 4, (z + 3) % 4, (z + 2) % 4

    def place(x, zz, c):
        return (replica, (x * 4 + zz) * 2 + c)

    x_peer = place(1 - x_hi, z, core)
    next_peer = place(x_hi, z_next, core)
    prev_peer = place(x_hi, z_prev, core)
    core_peer = place(x_hi, z, 1 - core)
    gossip_to = ((replica + distance) % REPLICAS, index)
    gossip_from = ((replica + REPLICAS - distance) % REPLICAS, index)

    def pair_rows(zz, c):
        return pl.ds(pl.multiple_of((zz * 2 + c) * 2 * unit, 2 * unit), 2 * unit)

    def unit_rows(zz, c, x):
        return pl.ds(pl.multiple_of((zz * 4 + c * 2 + x) * unit, unit), unit)

    def chunk_columns(k):
        return pl.ds(pl.multiple_of(k * CHUNK, CHUNK), CHUNK)

    hidden_load = pltpu.make_async_copy(hidden_hbm.at[0], token_hidden, load_sem.at[0])
    hidden_load.start()

    own_start = slot_of(index) * unit

    def own_load(k, part):
        return pltpu.make_async_copy(
            grads_hbm.at[0, part, :, chunk_columns(k)],
            gathered.at[k, pl.ds(pl.multiple_of(own_start + part * tokens, tokens), tokens)],
            own_sem.at[k, part],
        )

    def start_own(k, carry):
        for part in range(micro):
            own_load(k, part).start()
        return carry

    lax.fori_loop(0, chunks, start_own, 0)

    def param_loads(k):
        slot = k % 2
        return [
            pltpu.make_async_copy(
                source.at[0, :, chunk_columns(k)], target.at[slot], param_sem.at[slot, i]
            )
            for i, (source, target) in enumerate(
                (
                    (weight_hbm, weight_buf),
                    (moment_hbm, moment_buf),
                    (second_hbm, second_buf),
                )
            )
        ]

    for load in param_loads(0):
        load.start()

    barrier = pltpu.get_barrier_semaphore()

    def greet(s, carry):
        pl.semaphore_signal(
            barrier, 1, device_id=(replica, (index + s) % GROUP), device_id_type=MESH
        )
        return carry

    lax.fori_loop(1, GROUP, greet, 0)
    pl.semaphore_signal(barrier, 1, device_id=gossip_to, device_id_type=MESH)
    pl.semaphore_signal(barrier, 1, device_id=gossip_from, device_id_type=MESH)
    pl.semaphore_wait(barrier, GROUP - 1 + 2)

    def gather_copy(k, which, where, peer):
        return pltpu.make_async_remote_copy(
            src_ref=gathered.at[k, where],
            dst_ref=gathered.at[k, where],
            send_sem=gather_send.at[k, which],
            recv_sem=gather_recv.at[k, which],
            device_id=peer,
            device_id_type=MESH,
        )

    def stage_x(k):
        for part in range(micro):
            own_load(k, part).wait()
        gather_copy(k, TO_X, unit_rows(z, core, x_hi), x_peer).start()

    def stage_pair(k):
        gather_copy(k, TO_X, unit_rows(z, core, 1 - x_hi), x_peer).wait_recv()
        gather_copy(k, TO_NEXT, pair_rows(z, core), next_peer).start()
        gather_copy(k, TO_PREV, pair_rows(z, core), prev_peer).start()
        gather_copy(k, CORE_OWN, pair_rows(z, core), core_peer).start()

    def stage_forward(k):
        gather_copy(k, TO_NEXT, pair_rows(z_prev, core), next_peer).wait_recv()
        gather_copy(k, ON_NEXT, unit_rows(z_prev, core, 0), next_peer).start()
        gather_copy(k, TO_PREV, pair_rows(z_next, core), prev_peer).wait_recv()
        gather_copy(k, ON_PREV, unit_rows(z_next, core, 1), prev_peer).start()
        gather_copy(k, CORE_PREV, pair_rows(z_prev, core), core_peer).start()
        gather_copy(k, CORE_NEXT, pair_rows(z_next, core), core_peer).start()

    def stage_far(k):
        gather_copy(k, ON_NEXT, unit_rows(z_far, core, 0), next_peer).wait_recv()
        gather_copy(k, ON_PREV, unit_rows(z_far, core, 1), prev_peer).wait_recv()
        gather_copy(k, CORE_FAR, pair_rows(z_far, core), core_peer).start()

    def stage_core(k):
        for which, zz in (
            (CORE_OWN, z),
            (CORE_PREV, z_prev),
            (CORE_NEXT, z_next),
            (CORE_FAR, z_far),
        ):
            gather_copy(k, which, pair_rows(zz, 1 - core), core_peer).wait_recv()

    stage_x(0)
    stage_x(1)

    hidden_load.wait()

    def turn(b, carry):
        lanes = pl.ds(pl.multiple_of(b * LANES, LANES), LANES)
        block = token_hidden[:, :, lanes].reshape(unit, LANES)
        hidden_out[lanes, :] = block.T
        return carry

    lax.fori_loop(0, blocks, turn, 0)

    def hidden_rows(f):
        return pl.ds(pl.multiple_of(f * rows, 16), rows)

    def hidden_copy(s):
        peer = (index + s) % GROUP
        return pltpu.make_async_remote_copy(
            src_ref=hidden_out.at[hidden_rows(peer)],
            dst_ref=hidden_in.at[slot_of(index)],
            send_sem=hidden_send.at[s],
            recv_sem=hidden_recv.at[s],
            device_id=(replica, peer),
            device_id_type=MESH,
        )

    def hidden_start(s, carry):
        hidden_copy(s).start()
        return carry

    lax.fori_loop(1, GROUP, hidden_start, 0)

    def hidden_arrived(s, carry):
        owner = (index + GROUP - s) % GROUP
        slot = slot_of(owner)
        pltpu.make_async_remote_copy(
            src_ref=hidden_out.at[hidden_rows(index)],
            dst_ref=hidden_in.at[slot],
            send_sem=hidden_send.at[s],
            recv_sem=hidden_recv.at[s],
            device_id=(replica, owner),
            device_id_type=MESH,
        ).wait_recv()
        lanes = pl.ds(pl.multiple_of(slot * unit, unit), unit)
        hidden_t[:, lanes] = hidden_in[slot]
        return carry

    def gossip_copy(k):
        return pltpu.make_async_remote_copy(
            src_ref=stepped.at[k],
            dst_ref=partner.at[k],
            send_sem=gossip_send.at[k],
            recv_sem=gossip_recv.at[k],
            device_id=gossip_to,
            device_id_type=MESH,
        )

    def moment_store(k):
        return pltpu.make_async_copy(
            new_moment_buf.at[k % 2],
            new_moment_hbm.at[0, :, chunk_columns(k)],
            moment_out_sem.at[k % 2],
        )

    def weight_store(k):
        return pltpu.make_async_copy(
            new_weight_buf.at[k % 2],
            new_weight_hbm.at[0, :, chunk_columns(k)],
            weight_out_sem.at[k % 2],
        )

    bias_one = scale_ref[0]
    bias_two = scale_ref[1]

    def update(k):
        slot = k % 2
        for load in param_loads(k):
            load.wait()

        @pl.when(k + 1 < chunks)
        def _():
            for load in param_loads(k + 1):
                load.start()

        gradient = factor * jnp.dot(
            hidden_t[...], gathered[k], preferred_element_type=jnp.float32
        )

        @pl.when(k >= 2)
        def _():
            moment_store(k - 2).wait()

        first = beta_one * moment_buf[slot].astype(jnp.float32) + (1.0 - beta_one) * gradient
        new_moment_buf[slot] = first.astype(jnp.bfloat16)
        variance = (
            beta_two * second_buf[slot].astype(jnp.float32)
            + (1.0 - beta_two) * gradient * gradient
        )
        change = first / bias_one / (jnp.sqrt(variance / bias_two) + epsilon)
        wide = weight_buf[slot].astype(jnp.float32)
        stepped[k] = (wide - learn_rate * (change + decay_rate * wide)).astype(jnp.bfloat16)
        gossip_copy(k).start()
        moment_store(k).start()

    def cotangent(k):
        slot = k % 2
        part = lax.dot_general(
            weight_buf[slot],
            gathered[k],
            (((1,), (1,)), ((), ())),
            preferred_element_type=jnp.float32,
        )
        total[...] += part

    def step(i, carry):
        @pl.when(i + 2 < chunks)
        def _():
            stage_x(i + 2)

        @pl.when(i < chunks)
        def _():
            stage_pair(i)

        @pl.when((i >= 1) & (i - 1 < chunks))
        def _():
            stage_forward(i - 1)

        @pl.when((i >= 2) & (i - 2 < chunks))
        def _():
            stage_far(i - 2)

        @pl.when(i == 3)
        def _():
            lax.fori_loop(1, GROUP, hidden_arrived, 0)
            own_lanes = pl.ds(pl.multiple_of(slot_of(index) * unit, unit), unit)
            hidden_t[:, own_lanes] = hidden_out[hidden_rows(index)]
            total[...] = jnp.zeros_like(total)

        @pl.when(i >= 3)
        def _():
            stage_core(i - 3)
            update(i - 3)
            cotangent(i - 3)

        return carry

    lax.fori_loop(0, chunks + 3, step, 0)

    def back_copy(s):
        peer = (index + s) % GROUP
        return pltpu.make_async_remote_copy(
            src_ref=cotangent_out.at[peer],
            dst_ref=cotangent_in.at[hidden_rows(index)],
            send_sem=back_send.at[s],
            recv_sem=back_recv.at[s],
            device_id=(replica, peer),
            device_id_type=MESH,
        )

    def part_of(f):
        lanes = pl.ds(pl.multiple_of(slot_of(f) * unit, unit), unit)
        return (factor * total[:, lanes]).astype(jnp.bfloat16)

    def back_start(s, carry):
        peer = (index + s) % GROUP
        cotangent_out[peer] = part_of(peer)
        back_copy(s).start()
        return carry

    lax.fori_loop(1, GROUP, back_start, 0)
    cotangent_in[hidden_rows(index)] = part_of(index)

    def average(k, carry):
        gossip_copy(k).wait_recv()

        @pl.when(k >= 2)
        def _():
            weight_store(k - 2).wait()

        mean = 0.5 * (stepped[k].astype(jnp.float32) + partner[k].astype(jnp.float32))
        new_weight_buf[k % 2] = mean.astype(jnp.bfloat16)
        weight_store(k).start()
        return carry

    late = chunks - 4
    lax.fori_loop(0, late, average, 0)

    def back_arrived(s, carry):
        owner = (index + GROUP - s) % GROUP
        pltpu.make_async_remote_copy(
            src_ref=cotangent_out.at[owner],
            dst_ref=cotangent_in.at[hidden_rows(owner)],
            send_sem=back_send.at[s],
            recv_sem=back_recv.at[s],
            device_id=(replica, owner),
            device_id_type=MESH,
        ).wait_recv()
        return carry

    lax.fori_loop(1, GROUP, back_arrived, 0)

    def turn_back(b, carry):
        lanes = pl.ds(pl.multiple_of(b * LANES, LANES), LANES)
        block = cotangent_in[lanes, :].T
        token_hidden[:, :, lanes] = block.reshape(micro, tokens, LANES)
        return carry

    lax.fori_loop(0, blocks, turn_back, 0)
    hidden_grad_store = pltpu.make_async_copy(token_hidden, hidden_grad_hbm.at[0], load_sem.at[0])
    hidden_grad_store.start()

    lax.fori_loop(late, chunks, average, 0)

    def sent(k, carry):
        gather_copy(k, TO_X, unit_rows(z, core, x_hi), x_peer).wait_send()
        gather_copy(k, TO_NEXT, pair_rows(z, core), next_peer).wait_send()
        gather_copy(k, TO_PREV, pair_rows(z, core), prev_peer).wait_send()
        gather_copy(k, CORE_OWN, pair_rows(z, core), core_peer).wait_send()
        gather_copy(k, ON_NEXT, unit_rows(z_prev, core, 0), next_peer).wait_send()
        gather_copy(k, ON_PREV, unit_rows(z_next, core, 1), prev_peer).wait_send()
        gather_copy(k, CORE_PREV, pair_rows(z_prev, core), core_peer).wait_send()
        gather_copy(k, CORE_NEXT, pair_rows(z_next, core), core_peer).wait_send()
        gather_copy(k, CORE_FAR, pair_rows(z_far, core), core_peer).wait_send()
        gossip_copy(k).wait_send()
        return carry

    lax.fori_loop(0, chunks, sent, 0)

    def exchanged(s, carry):
        hidden_copy(s).wait_send()
        back_copy(s).wait_send()
        return carry

    lax.fori_loop(1, GROUP, exchanged, 0)
    for k in (chunks - 2, chunks - 1):
        moment_store(k).wait()
        weight_store(k).wait()
    hidden_grad_store.wait()


def step_call(level, factor, scale, hidden, out_grad, weight, moment, second):
    _, micro, tokens, width = hidden.shape
    _, rows, depth = weight.shape
    chunks = depth // CHUNK
    unit = micro * tokens
    half = jnp.bfloat16
    anywhere = pl.BlockSpec(memory_space=pl.ANY)
    scratch = [
        pltpu.VMEM((chunks, GROUP * unit, CHUNK), half),
        pltpu.VMEM((micro, tokens, width), half),
        pltpu.VMEM((width, unit), half),
        pltpu.VMEM((GROUP, rows, unit), half),
        pltpu.VMEM((rows, GROUP * unit), half),
        pltpu.VMEM((rows, GROUP * unit), jnp.float32),
        pltpu.VMEM((chunks, rows, CHUNK), half),
        pltpu.VMEM((chunks, rows, CHUNK), half),
        pltpu.VMEM((GROUP, rows, unit), half),
        pltpu.VMEM((width, unit), half),
        pltpu.VMEM((2, rows, CHUNK), half),
        pltpu.VMEM((2, rows, CHUNK), half),
        pltpu.VMEM((2, rows, CHUNK), half),
        pltpu.VMEM((2, rows, CHUNK), half),
        pltpu.VMEM((2, rows, CHUNK), half),
        pltpu.SemaphoreType.DMA((1,)),
        pltpu.SemaphoreType.DMA((chunks, micro)),
        pltpu.SemaphoreType.DMA((2, 3)),
        pltpu.SemaphoreType.DMA((2,)),
        pltpu.SemaphoreType.DMA((2,)),
        pltpu.SemaphoreType.DMA((chunks, COPIES)),
        pltpu.SemaphoreType.DMA((chunks, COPIES)),
        pltpu.SemaphoreType.DMA((GROUP,)),
        pltpu.SemaphoreType.DMA((GROUP,)),
        pltpu.SemaphoreType.DMA((GROUP,)),
        pltpu.SemaphoreType.DMA((GROUP,)),
        pltpu.SemaphoreType.DMA((chunks,)),
        pltpu.SemaphoreType.DMA((chunks,)),
    ]
    products = 2 * GROUP * unit * rows * depth
    return pl.pallas_call(
        functools.partial(step_kernel, 1 << level, factor),
        out_shape=(
            jax.ShapeDtypeStruct(weight.shape, half),
            jax.ShapeDtypeStruct(moment.shape, half),
            jax.ShapeDtypeStruct(hidden.shape, half),
        ),
        in_specs=[pl.BlockSpec(memory_space=pltpu.SMEM)] + [anywhere] * 5,
        out_specs=(anywhere,) * 3,
        scratch_shapes=scratch,
        name=f"step_{1 << level}",
        cost_estimate=pl.CostEstimate(
            flops=2 * products,
            bytes_accessed=2 * (2 * hidden.size + out_grad.size + 5 * weight.size),
            transcendentals=weight.size,
        ),
        compiler_params=pltpu.CompilerParams(
            collective_id=level, has_side_effects=True, vmem_limit_bytes=60 * 2**20
        ),
    )(scale, hidden, out_grad, weight, moment, second)


def on_device(step_index, hidden, out_grad, weight, moment, second):
    factor = hidden.shape[3] ** (-0.5)
    step_float = step_index.astype(jnp.float32)
    scale = jnp.stack([1.0 - beta_one**step_float, 1.0 - beta_two**step_float])
    levels = REPLICAS.bit_length() - 1
    branches = [functools.partial(step_call, level, factor) for level in range(levels)]
    return lax.switch(
        step_index % levels, branches, scale, hidden, out_grad, weight, moment, second
    )


def solution(mesh):
    placed = (
        P(),
        P("replica", None, "fsdp", None),
        P("replica", None, "fsdp", None),
        P("replica", "fsdp", None),
        P("replica", "fsdp", None),
        P("replica", "fsdp", None),
    )
    return jax.shard_map(
        on_device,
        mesh=mesh,
        in_specs=placed,
        out_specs=(
            P("replica", "fsdp", None),
            P("replica", "fsdp", None),
            P("replica", None, "fsdp", None),
        ),
        check_vma=False,
    )
```

time: 368 us -> 206 us (0.56); the launches traced: 363 us -> 206 us
  waiting for transfers between devices: 238 us -> 0 us
  Pallas kernels: 0 us -> 196 us
  matrix products: 53 us -> 0 us
  starting transfers between devices: 27.9 us -> 0 us
  between operations: 14.8 us -> 1.39 us
  local copies, waits for them, and re-layouts: 19.3 us -> 8.08 us
  other arithmetic: 9.76 us -> 0.08 us
    pallas_call x0 -> x1, Pallas kernels: none -> 196 us  [step_call(): pl.pallas_call(functools.partial(step_kernel, 1 << level, factor), out_sh...]
    all_gather x2 -> x0, waiting for transfers between devices: 128 us -> none  [gradient_rows(): gathered = lax.all_gather(token_grads, 'fsdp', axis=0, tiled=True)]
    ppermute x1 -> x0, waiting for transfers between devices: 96.3 us -> none  [shifted(): return lax.ppermute(block, axis, route)]
    dot_general x4 -> x0, matrix products: 53 us -> none  [the longest x2 33 us: gradient_rows(): lax.dot_general(spread_rows, gathered, (((0,), (0,)), ((), ())), preferre...]
    all_to_all x4 -> x0, starting transfers between devices: 26.9 us -> none  [the longest x2 13.8 us: return_rows(): lax.all_to_all(hidden_part, 'fsdp', split_axis=0, concat_axis=1, tiled=True)]
    all_to_all x4 -> x0, waiting for transfers between devices: 13.2 us -> none  [the longest x2 6.91 us: gradient_rows(): lax.all_to_all(token_hidden, 'fsdp', split_axis=1, concat_axis=0, tiled=T...]
    all_to_all x6 -> x0, local copies, waits for them, and re-layouts: 8.79 us -> none  [the longest x4 7.63 us: gradient_rows(): lax.all_to_all(token_hidden, 'fsdp', split_axis=1, concat_axis=0, tiled=T...]
    unnamed x0 -> x5, local copies, waits for them, and re-layouts: none -> 8.08 us
  transfers between devices with their start and end apart: 7 -> 0, of which waited for: 5 -> 0; matrix products, arithmetic and copies ran while one was open for 19% -> 0% of each run, Pallas kernels for 0% -> 0%
where the time goes in v1:
time: 206 us
  Pallas kernels  196 us (95%)
  local copies, waits for them, and re-layouts  8.08 us (4%)
    pallas_call x1, Pallas kernels, step_call(): pl.pallas_call(functools.partial(step_kernel, 1 << level, factor), out_sh...  196 us
    unnamed x5, local copies, waits for them, and re-layouts  8.08 us

profile of v1, /device:TPU:113, one launch (start us, length us, event | category | flops | bytes accessed | tf_op | source)
XLA Modules:
  0.0 206.3 jit_solution(11881244561033169463)
XLA Ops:
  1.4 0.1 pad_maximum_fusion
  1.5 196.7 %conditional.1 = ((bf16[1,432,5120]{2,1,0:T(8,128)(2,1)}, bf16[1,432,5120]{2,1,0:T(8,128)(2,1)}, bf16[1,2,64,6912]{3,2,1,0:T(8,128)(2,1)S(1)})) conditional(s32[]{:T(128)} %clamp.3, (f32[2]{0:T(128)S(1)}, bf16[1,2,64,6912]{3,2,1,0:T(8,128)(2,1)}, bf16[1,2,64,5120]{3,2,1,0:T(8,128)(2,1)}, bf16[1,432,5120]{2,1,0:T(8,128)(2,1)}, ...), branch_computations={%region_0.1_spmd, %region_1.2_spmd, %region_2.3_spmd} | conditional | flops 18119393280 | bytes 26968072 | solution.py:503
  1.5 196.3 %step_2.1 = (bf16[1,432,5120]{2,1,0:T(8,128)(2,1)}, bf16[1,432,5120]{2,1,0:T(8,128)(2,1)}, bf16[1,2,64,6912]{3,2,1,0:T(8,128)(2,1)S(1)}) custom-call(f32[2]{0:T(128)S(1)} %get-tuple-element.42.scale_ref, bf16[1,2,64,6912]{3,2,1,0:T(8,128)(2,1)} %get-tuple-element.85.hidden_hbm, bf16[1,2,64,5120]{3,2,1,0:T(8,128)(2,1)} %get-tuple-element.88.grads_hbm, ...), custom_call_target="tpu_custom_call" | custom-call | flops 18119393280 | bytes 26968064 | tf_op jit(solution)/shard_map/cond/branch_1_fun/step_2/pallas_call | solution.py:475
  198.2 0.0 copy-start
  198.2 4.8 %copy.46 = bf16[1,432,5120]{2,1,0:T(8,128)(2,1)} copy(bf16[1,432,5120]{2,1,0:T(8,128)(2,1)} %get-tuple-element.111) | data formatting | bytes 8847360
  203.0 0.0 copy-done
  203.0 2.1 %copy.47 = bf16[1,432,5120]{2,1,0:T(8,128)(2,1)} copy(bf16[1,432,5120]{2,1,0:T(8,128)(2,1)S(1)} %copy-done) | data formatting | bytes 8847360
  205.1 1.2 copy.48
Async XLA Ops:
  198.2 4.8 %copy-start = (bf16[1,432,5120]{2,1,0:T(8,128)(2,1)S(1)}, bf16[1,432,5120]{2,1,0:T(8,128)(2,1)}, u32[]{:S(2)}) copy-start(bf16[1,432,5120]{2,1,0:T(8,128)(2,1)} %get-tuple-element.112) | copy-start | bytes 13271044

commit v2 on v1

--- a/solution.py
+++ b/solution.py
@@ -18,6 +18,9 @@
 REPLICAS = 8
 LANES = 128
 CHUNK = 256
+EARLY = 6
+RELAY_LAG = 6
+TURNS = 6
 
 TO_X, TO_NEXT, TO_PREV, CORE_OWN, ON_NEXT, ON_PREV, CORE_PREV, CORE_NEXT, CORE_FAR = range(9)
 COPIES = 9
@@ -54,7 +57,7 @@
     moment_buf,
     second_buf,
     new_moment_buf,
-    new_weight_buf,
+    relayed,
     load_sem,
     own_sem,
     param_sem,
@@ -68,6 +71,8 @@
     back_recv,
     gossip_send,
     gossip_recv,
+    relay_send,
+    relay_recv,
 ):
     chunks = gathered.shape[0]
     rows = weight_buf.shape[1]
@@ -90,6 +95,14 @@
     core_peer = place(x_hi, z, 1 - core)
     gossip_to = ((replica + distance) % REPLICAS, index)
     gossip_from = ((replica + REPLICAS - distance) % REPLICAS, index)
+
+    x_lo, y = replica // 4, replica % 4
+    relays = relayed.shape[0] if distance < 4 else 0
+    wraps = y >= 4 - distance
+    lands = y < distance
+    y_ahead = (x_lo * 4 + (y + distance) % 4, index)
+    y_behind = (x_lo * 4 + (y + 4 - distance) % 4, index)
+    x_beside = ((1 - x_lo) * 4 + y, index)
 
     def pair_rows(zz, c):
         return pl.ds(pl.multiple_of((zz * 2 + c) * 2 * unit, 2 * unit), 2 * unit)
@@ -148,7 +161,12 @@
     lax.fori_loop(1, GROUP, greet, 0)
     pl.semaphore_signal(barrier, 1, device_id=gossip_to, device_id_type=MESH)
     pl.semaphore_signal(barrier, 1, device_id=gossip_from, device_id_type=MESH)
-    pl.semaphore_wait(barrier, GROUP - 1 + 2)
+    greeted = GROUP - 1 + 2
+    if relays:
+        for peer in (y_ahead, y_behind, x_beside):
+            pl.semaphore_signal(barrier, 1, device_id=peer, device_id_type=MESH)
+        greeted += 3
+    pl.semaphore_wait(barrier, greeted)
 
     def gather_copy(k, which, where, peer):
         return pltpu.make_async_remote_copy(
@@ -199,12 +217,13 @@
     hidden_load.wait()
 
     def turn(b, carry):
-        lanes = pl.ds(pl.multiple_of(b * LANES, LANES), LANES)
-        block = token_hidden[:, :, lanes].reshape(unit, LANES)
-        hidden_out[lanes, :] = block.T
-        return carry
-
-    lax.fori_loop(0, blocks, turn, 0)
+        for t in range(TURNS):
+            lanes = pl.ds(pl.multiple_of((b * TURNS + t) * LANES, LANES), LANES)
+            block = token_hidden[:, :, lanes].reshape(unit, LANES)
+            hidden_out[lanes, :] = block.T
+        return carry
+
+    lax.fori_loop(0, blocks // TURNS, turn, 0)
 
     def hidden_rows(f):
         return pl.ds(pl.multiple_of(f * rows, 16), rows)
@@ -225,6 +244,12 @@
         return carry
 
     lax.fori_loop(1, GROUP, hidden_start, 0)
+
+    def exchange(k, carry):
+        stage_x(k)
+        return carry
+
+    lax.fori_loop(2, EARLY, exchange, 0)
 
     def hidden_arrived(s, carry):
         owner = (index + GROUP - s) % GROUP
@@ -251,6 +276,45 @@
             device_id_type=MESH,
         )
 
+    def relay_copy(k, peer):
+        return pltpu.make_async_remote_copy(
+            src_ref=stepped.at[k],
+            dst_ref=relayed.at[k // 2],
+            send_sem=gossip_send.at[k],
+            recv_sem=relay_recv.at[k // 2],
+            device_id=peer,
+            device_id_type=MESH,
+        )
+
+    def pass_on_copy(k, peer):
+        return pltpu.make_async_remote_copy(
+            src_ref=relayed.at[k // 2],
+            dst_ref=partner.at[k],
+            send_sem=relay_send.at[k // 2],
+            recv_sem=gossip_recv.at[k],
+            device_id=peer,
+            device_id_type=MESH,
+        )
+
+    def gossip_start(k):
+        if relays:
+            by_relay = wraps & (k // 2 < relays)
+
+            @pl.when(by_relay & (k % 2 == 0))
+            def _():
+                relay_copy(k, y_ahead).start()
+
+            @pl.when(by_relay & (k % 2 == 1))
+            def _():
+                relay_copy(k, x_beside).start()
+
+            @pl.when(jnp.logical_not(by_relay))
+            def _():
+                gossip_copy(k).start()
+
+        else:
+            gossip_copy(k).start()
+
     def moment_store(k):
         return pltpu.make_async_copy(
             new_moment_buf.at[k % 2],
@@ -260,9 +324,9 @@
 
     def weight_store(k):
         return pltpu.make_async_copy(
-            new_weight_buf.at[k % 2],
+            partner.at[k],
             new_weight_hbm.at[0, :, chunk_columns(k)],
-            weight_out_sem.at[k % 2],
+            weight_out_sem.at[k],
         )
 
     bias_one = scale_ref[0]
@@ -295,7 +359,7 @@
         change = first / bias_one / (jnp.sqrt(variance / bias_two) + epsilon)
         wide = weight_buf[slot].astype(jnp.float32)
         stepped[k] = (wide - learn_rate * (change + decay_rate * wide)).astype(jnp.bfloat16)
-        gossip_copy(k).start()
+        gossip_start(k)
         moment_store(k).start()
 
     def cotangent(k):
@@ -309,10 +373,6 @@
         total[...] += part
 
     def step(i, carry):
-        @pl.when(i + 2 < chunks)
-        def _():
-            stage_x(i + 2)
-
         @pl.when(i < chunks)
         def _():
             stage_pair(i)
@@ -331,16 +391,30 @@
             own_lanes = pl.ds(pl.multiple_of(slot_of(index) * unit, unit), unit)
             hidden_t[:, own_lanes] = hidden_out[hidden_rows(index)]
             total[...] = jnp.zeros_like(total)
-
-        @pl.when(i >= 3)
+            lax.fori_loop(EARLY, chunks, exchange, 0)
+
+        @pl.when((i >= 3) & (i - 3 < chunks))
         def _():
             stage_core(i - 3)
             update(i - 3)
             cotangent(i - 3)
 
-        return carry
-
-    lax.fori_loop(0, chunks + 3, step, 0)
+        if relays:
+            late = i - RELAY_LAG
+
+            @pl.when(lands & (late >= 0) & (late % 2 == 0) & (late // 2 < relays))
+            def _():
+                relay_copy(late, x_beside).wait_recv()
+                pass_on_copy(late, x_beside).start()
+
+            @pl.when(wraps & (late >= 0) & (late % 2 == 1) & (late // 2 < relays))
+            def _():
+                relay_copy(late, x_beside).wait_recv()
+                pass_on_copy(late, y_ahead).start()
+
+        return carry
+
+    lax.fori_loop(0, chunks + 4, step, 0)
 
     def back_copy(s):
         peer = (index + s) % GROUP
@@ -368,13 +442,8 @@
 
     def average(k, carry):
         gossip_copy(k).wait_recv()
-
-        @pl.when(k >= 2)
-        def _():
-            weight_store(k - 2).wait()
-
         mean = 0.5 * (stepped[k].astype(jnp.float32) + partner[k].astype(jnp.float32))
-        new_weight_buf[k % 2] = mean.astype(jnp.bfloat16)
+        partner[k] = mean.astype(jnp.bfloat16)
         weight_store(k).start()
         return carry
 
@@ -396,12 +465,13 @@
     lax.fori_loop(1, GROUP, back_arrived, 0)
 
     def turn_back(b, carry):
-        lanes = pl.ds(pl.multiple_of(b * LANES, LANES), LANES)
-        block = cotangent_in[lanes, :].T
-        token_hidden[:, :, lanes] = block.reshape(micro, tokens, LANES)
-        return carry
-
-    lax.fori_loop(0, blocks, turn_back, 0)
+        for t in range(TURNS):
+            lanes = pl.ds(pl.multiple_of((b * TURNS + t) * LANES, LANES), LANES)
+            block = cotangent_in[lanes, :].T
+            token_hidden[:, :, lanes] = block.reshape(micro, tokens, LANES)
+        return carry
+
+    lax.fori_loop(0, blocks // TURNS, turn_back, 0)
     hidden_grad_store = pltpu.make_async_copy(token_hidden, hidden_grad_hbm.at[0], load_sem.at[0])
     hidden_grad_store.start()
 
@@ -418,6 +488,7 @@
         gather_copy(k, CORE_NEXT, pair_rows(z_next, core), core_peer).wait_send()
         gather_copy(k, CORE_FAR, pair_rows(z_far, core), core_peer).wait_send()
         gossip_copy(k).wait_send()
+        weight_store(k).wait()
         return carry
 
     lax.fori_loop(0, chunks, sent, 0)
@@ -430,7 +501,16 @@
     lax.fori_loop(1, GROUP, exchanged, 0)
     for k in (chunks - 2, chunks - 1):
         moment_store(k).wait()
-        weight_store(k).wait()
+    if relays:
+
+        @pl.when(lands | wraps)
+        def _():
+            def passed(j, carry):
+                pass_on_copy(2 * j, x_beside).wait_send()
+                return carry
+
+            lax.fori_loop(0, relays, passed, 0)
+
     hidden_grad_store.wait()
 
 
@@ -439,6 +519,7 @@
     _, rows, depth = weight.shape
     chunks = depth // CHUNK
     unit = micro * tokens
+    relays = chunks // 2 - 1
     half = jnp.bfloat16
     anywhere = pl.BlockSpec(memory_space=pl.ANY)
     scratch = [
@@ -456,12 +537,12 @@
         pltpu.VMEM((2, rows, CHUNK), half),
         pltpu.VMEM((2, rows, CHUNK), half),
         pltpu.VMEM((2, rows, CHUNK), half),
-        pltpu.VMEM((2, rows, CHUNK), half),
+        pltpu.VMEM((relays, rows, CHUNK), half),
         pltpu.SemaphoreType.DMA((1,)),
         pltpu.SemaphoreType.DMA((chunks, micro)),
         pltpu.SemaphoreType.DMA((2, 3)),
         pltpu.SemaphoreType.DMA((2,)),
-        pltpu.SemaphoreType.DMA((2,)),
+        pltpu.SemaphoreType.DMA((chunks,)),
         pltpu.SemaphoreType.DMA((chunks, COPIES)),
         pltpu.SemaphoreType.DMA((chunks, COPIES)),
         pltpu.SemaphoreType.DMA((GROUP,)),
@@ -470,6 +551,8 @@
         pltpu.SemaphoreType.DMA((GROUP,)),
         pltpu.SemaphoreType.DMA((chunks,)),
         pltpu.SemaphoreType.DMA((chunks,)),
+        pltpu.SemaphoreType.DMA((relays,)),
+        pltpu.SemaphoreType.DMA((relays,)),
     ]
     products = 2 * GROUP * unit * rows * depth
     return pl.pallas_call(
@@ -489,7 +572,7 @@
             transcendentals=weight.size,
         ),
         compiler_params=pltpu.CompilerParams(
-            collective_id=level, has_side_effects=True, vmem_limit_bytes=60 * 2**20
+            collective_id=level, has_side_effects=True, vmem_limit_bytes=50 * 2**20
         ),
     )(scale, hidden, out_grad, weight, moment, second)
 

time: 206 us -> 199 us (0.966)
  Pallas kernels: 196 us -> 188 us
    pallas_call x1, Pallas kernels: 196 us -> 188 us  [step_call(): pl.pallas_call(functools.partial(step_kernel, 1 << level, factor), out_sh...]
where the time goes in v2:
time: 199 us; the launch traced here: 198 us
  Pallas kernels  188 us (94%)
  local copies, waits for them, and re-layouts  8.08 us (4%)
    pallas_call x1, Pallas kernels, step_call(): pl.pallas_call(functools.partial(step_kernel, 1 << level, factor), out_sh...  188 us
    unnamed x5, local copies, waits for them, and re-layouts  8.08 us

profile of v2, /device:TPU:113, one launch (start us, length us, event | category | flops | bytes accessed | tf_op | source)
XLA Modules:
  0.0 197.8 jit_solution(13853883320694393127)
XLA Ops:
  1.4 0.1 pad_maximum_fusion
  1.5 188.3 %conditional.1 = ((bf16[1,432,5120]{2,1,0:T(8,128)(2,1)}, bf16[1,432,5120]{2,1,0:T(8,128)(2,1)}, bf16[1,2,64,6912]{3,2,1,0:T(8,128)(2,1)S(1)})) conditional(s32[]{:T(128)} %clamp.3, (f32[2]{0:T(128)S(1)}, bf16[1,2,64,6912]{3,2,1,0:T(8,128)(2,1)}, bf16[1,2,64,5120]{3,2,1,0:T(8,128)(2,1)}, bf16[1,432,5120]{2,1,0:T(8,128)(2,1)}, ...), branch_computations={%region_0.1_spmd, %region_1.2_spmd, %region_2.3_spmd} | conditional | flops 18119393280 | bytes 26968072 | solution.py:586
  1.6 187.9 %step_4.1 = (bf16[1,432,5120]{2,1,0:T(8,128)(2,1)}, bf16[1,432,5120]{2,1,0:T(8,128)(2,1)}, bf16[1,2,64,6912]{3,2,1,0:T(8,128)(2,1)S(1)}) custom-call(f32[2]{0:T(128)S(1)} %get-tuple-element.48.scale_ref, bf16[1,2,64,6912]{3,2,1,0:T(8,128)(2,1)} %get-tuple-element.86.hidden_hbm, bf16[1,2,64,5120]{3,2,1,0:T(8,128)(2,1)} %get-tuple-element.89.grads_hbm, ...), custom_call_target="tpu_custom_call" | custom-call | flops 18119393280 | bytes 26968064 | tf_op jit(solution)/shard_map/cond/branch_2_fun/step_4/pallas_call | solution.py:558
  189.7 0.0 copy-start
  189.8 4.8 %copy.46 = bf16[1,432,5120]{2,1,0:T(8,128)(2,1)} copy(bf16[1,432,5120]{2,1,0:T(8,128)(2,1)} %get-tuple-element.111) | data formatting | bytes 8847360
  194.5 0.0 copy-done
  194.5 2.1 %copy.47 = bf16[1,432,5120]{2,1,0:T(8,128)(2,1)} copy(bf16[1,432,5120]{2,1,0:T(8,128)(2,1)S(1)} %copy-done) | data formatting | bytes 8847360
  196.6 1.2 copy.48
Async XLA Ops:
  189.7 4.8 %copy-start = (bf16[1,432,5120]{2,1,0:T(8,128)(2,1)S(1)}, bf16[1,432,5120]{2,1,0:T(8,128)(2,1)}, u32[]{:S(2)}) copy-start(bf16[1,432,5120]{2,1,0:T(8,128)(2,1)} %get-tuple-element.112) | copy-start | bytes 13271044

commit v3 on v2

--- a/solution.py
+++ b/solution.py
@@ -18,8 +18,8 @@
 REPLICAS = 8
 LANES = 128
 CHUNK = 256
-EARLY = 6
-RELAY_LAG = 6
+EARLY = 8
+FORWARD, FAR, USE, RELAY = 2, 4, 5, 8
 TURNS = 6
 
 TO_X, TO_NEXT, TO_PREV, CORE_OWN, ON_NEXT, ON_PREV, CORE_PREV, CORE_NEXT, CORE_FAR = range(9)
@@ -225,11 +225,17 @@
 
     lax.fori_loop(0, blocks // TURNS, turn, 0)
 
+    def ahead(s):
+        return ((x_hi + s // 8) % 2 * 4 + (z + (s // 2) % 4) % 4) * 2 + (core + s) % 2
+
+    def behind(s):
+        return ((x_hi + s // 8) % 2 * 4 + (z + 4 - (s // 2) % 4) % 4) * 2 + (core + s) % 2
+
     def hidden_rows(f):
         return pl.ds(pl.multiple_of(f * rows, 16), rows)
 
     def hidden_copy(s):
-        peer = (index + s) % GROUP
+        peer = ahead(s)
         return pltpu.make_async_remote_copy(
             src_ref=hidden_out.at[hidden_rows(peer)],
             dst_ref=hidden_in.at[slot_of(index)],
@@ -240,7 +246,7 @@
         )
 
     def hidden_start(s, carry):
-        hidden_copy(s).start()
+        hidden_copy(GROUP - s).start()
         return carry
 
     lax.fori_loop(1, GROUP, hidden_start, 0)
@@ -252,7 +258,7 @@
     lax.fori_loop(2, EARLY, exchange, 0)
 
     def hidden_arrived(s, carry):
-        owner = (index + GROUP - s) % GROUP
+        owner = behind(s)
         slot = slot_of(owner)
         pltpu.make_async_remote_copy(
             src_ref=hidden_out.at[hidden_rows(index)],
@@ -279,36 +285,39 @@
     def relay_copy(k, peer):
         return pltpu.make_async_remote_copy(
             src_ref=stepped.at[k],
-            dst_ref=relayed.at[k // 2],
+            dst_ref=relayed.at[k % relays],
             send_sem=gossip_send.at[k],
-            recv_sem=relay_recv.at[k // 2],
+            recv_sem=relay_recv.at[k % relays],
             device_id=peer,
             device_id_type=MESH,
         )
 
     def pass_on_copy(k, peer):
         return pltpu.make_async_remote_copy(
-            src_ref=relayed.at[k // 2],
+            src_ref=relayed.at[k % relays],
             dst_ref=partner.at[k],
-            send_sem=relay_send.at[k // 2],
+            send_sem=relay_send.at[k % relays],
             recv_sem=gossip_recv.at[k],
             device_id=peer,
             device_id_type=MESH,
         )
 
+    def pass_on(k, peer):
+        relay_copy(k, x_beside).wait_recv()
+        pass_on_copy(k, peer).start()
+
     def gossip_start(k):
         if relays:
-            by_relay = wraps & (k // 2 < relays)
-
-            @pl.when(by_relay & (k % 2 == 0))
+
+            @pl.when(wraps & (k < relays))
             def _():
                 relay_copy(k, y_ahead).start()
 
-            @pl.when(by_relay & (k % 2 == 1))
+            @pl.when(wraps & (k >= relays))
             def _():
                 relay_copy(k, x_beside).start()
 
-            @pl.when(jnp.logical_not(by_relay))
+            @pl.when(jnp.logical_not(wraps))
             def _():
                 gossip_copy(k).start()
 
@@ -377,15 +386,11 @@
         def _():
             stage_pair(i)
 
-        @pl.when((i >= 1) & (i - 1 < chunks))
-        def _():
-            stage_forward(i - 1)
-
-        @pl.when((i >= 2) & (i - 2 < chunks))
-        def _():
-            stage_far(i - 2)
-
-        @pl.when(i == 3)
+        @pl.when((i >= FORWARD) & (i - FORWARD < chunks))
+        def _():
+            stage_forward(i - FORWARD)
+
+        @pl.when(i == USE)
         def _():
             lax.fori_loop(1, GROUP, hidden_arrived, 0)
             own_lanes = pl.ds(pl.multiple_of(slot_of(index) * unit, unit), unit)
@@ -393,31 +398,36 @@
             total[...] = jnp.zeros_like(total)
             lax.fori_loop(EARLY, chunks, exchange, 0)
 
-        @pl.when((i >= 3) & (i - 3 < chunks))
-        def _():
-            stage_core(i - 3)
-            update(i - 3)
-            cotangent(i - 3)
+        @pl.when((i >= USE) & (i - USE < chunks))
+        def _():
+            stage_core(i - USE)
+            update(i - USE)
+
+        @pl.when((i >= FAR) & (i - FAR < chunks))
+        def _():
+            stage_far(i - FAR)
+
+        @pl.when((i >= USE) & (i - USE < chunks))
+        def _():
+            cotangent(i - USE)
 
         if relays:
-            late = i - RELAY_LAG
-
-            @pl.when(lands & (late >= 0) & (late % 2 == 0) & (late // 2 < relays))
+            over_y, over_x = i - RELAY, i - USE - 1
+
+            @pl.when(lands & (over_y >= 0) & (over_y < relays))
             def _():
-                relay_copy(late, x_beside).wait_recv()
-                pass_on_copy(late, x_beside).start()
-
-            @pl.when(wraps & (late >= 0) & (late % 2 == 1) & (late // 2 < relays))
+                pass_on(over_y, x_beside)
+
+            @pl.when(wraps & (over_x >= relays))
             def _():
-                relay_copy(late, x_beside).wait_recv()
-                pass_on_copy(late, y_ahead).start()
-
-        return carry
-
-    lax.fori_loop(0, chunks + 4, step, 0)
+                pass_on(over_x, y_ahead)
+
+        return carry
+
+    lax.fori_loop(0, chunks + USE, step, 0)
 
     def back_copy(s):
-        peer = (index + s) % GROUP
+        peer = ahead(s)
         return pltpu.make_async_remote_copy(
             src_ref=cotangent_out.at[peer],
             dst_ref=cotangent_in.at[hidden_rows(index)],
@@ -432,13 +442,19 @@
         return (factor * total[:, lanes]).astype(jnp.bfloat16)
 
     def back_start(s, carry):
-        peer = (index + s) % GROUP
+        peer = ahead(GROUP - s)
         cotangent_out[peer] = part_of(peer)
-        back_copy(s).start()
+        back_copy(GROUP - s).start()
         return carry
 
     lax.fori_loop(1, GROUP, back_start, 0)
     cotangent_in[hidden_rows(index)] = part_of(index)
+    if relays:
+
+        @pl.when(wraps)
+        def _():
+            pass_on(chunks - 1, y_ahead)
+
 
     def average(k, carry):
         gossip_copy(k).wait_recv()
@@ -451,7 +467,7 @@
     lax.fori_loop(0, late, average, 0)
 
     def back_arrived(s, carry):
-        owner = (index + GROUP - s) % GROUP
+        owner = behind(s)
         pltpu.make_async_remote_copy(
             src_ref=cotangent_out.at[owner],
             dst_ref=cotangent_in.at[hidden_rows(owner)],
@@ -506,7 +522,7 @@
         @pl.when(lands | wraps)
         def _():
             def passed(j, carry):
-                pass_on_copy(2 * j, x_beside).wait_send()
+                pass_on_copy(j, x_beside).wait_send()
                 return carry
 
             lax.fori_loop(0, relays, passed, 0)
@@ -519,7 +535,7 @@
     _, rows, depth = weight.shape
     chunks = depth // CHUNK
     unit = micro * tokens
-    relays = chunks // 2 - 1
+    relays = chunks // 2
     half = jnp.bfloat16
     anywhere = pl.BlockSpec(memory_space=pl.ANY)
     scratch = [

time: 199 us -> 172 us (0.86)
  Pallas kernels: 188 us -> 159 us
    pallas_call x1, Pallas kernels: 188 us -> 159 us  [step_call(): pl.pallas_call(functools.partial(step_kernel, 1 << level, factor), out_sh...]
where the time goes in v3:
time: 172 us; the launch traced here: 169 us
  Pallas kernels  159 us (92%)
  local copies, waits for them, and re-layouts  8.08 us (5%)
    pallas_call x1, Pallas kernels, step_call(): pl.pallas_call(functools.partial(step_kernel, 1 << level, factor), out_sh...  159 us
    unnamed x5, local copies, waits for them, and re-layouts  8.08 us

profile of v3, /device:TPU:113, one launch (start us, length us, event | category | flops | bytes accessed | tf_op | source)
XLA Modules:
  0.0 169.0 jit_solution(6899837695253959912)
XLA Ops:
  1.4 0.1 pad_maximum_fusion
  1.5 159.4 %conditional.1 = ((bf16[1,432,5120]{2,1,0:T(8,128)(2,1)}, bf16[1,432,5120]{2,1,0:T(8,128)(2,1)}, bf16[1,2,64,6912]{3,2,1,0:T(8,128)(2,1)S(1)})) conditional(s32[]{:T(128)} %clamp.3, (f32[2]{0:T(128)S(1)}, bf16[1,2,64,6912]{3,2,1,0:T(8,128)(2,1)}, bf16[1,2,64,5120]{3,2,1,0:T(8,128)(2,1)}, bf16[1,432,5120]{2,1,0:T(8,128)(2,1)}, ...), branch_computations={%region_0.1_spmd, %region_1.2_spmd, %region_2.3_spmd} | conditional | flops 18119393280 | bytes 26968072 | solution.py:602
  1.5 159.4 %step_2.1 = (bf16[1,432,5120]{2,1,0:T(8,128)(2,1)}, bf16[1,432,5120]{2,1,0:T(8,128)(2,1)}, bf16[1,2,64,6912]{3,2,1,0:T(8,128)(2,1)S(1)}) custom-call(f32[2]{0:T(128)S(1)} %get-tuple-element.42.scale_ref, bf16[1,2,64,6912]{3,2,1,0:T(8,128)(2,1)} %get-tuple-element.85.hidden_hbm, bf16[1,2,64,5120]{3,2,1,0:T(8,128)(2,1)} %get-tuple-element.88.grads_hbm, ...), custom_call_target="tpu_custom_call" | custom-call | flops 18119393280 | bytes 26968064 | tf_op jit(solution)/shard_map/cond/branch_1_fun/step_2/pallas_call | solution.py:574
  160.9 0.0 copy-start
  160.9 4.8 %copy.46 = bf16[1,432,5120]{2,1,0:T(8,128)(2,1)} copy(bf16[1,432,5120]{2,1,0:T(8,128)(2,1)} %get-tuple-element.111) | data formatting | bytes 8847360
  165.7 0.0 copy-done
  165.7 2.1 %copy.47 = bf16[1,432,5120]{2,1,0:T(8,128)(2,1)} copy(bf16[1,432,5120]{2,1,0:T(8,128)(2,1)S(1)} %copy-done) | data formatting | bytes 8847360
  167.8 1.2 copy.48
Async XLA Ops:
  160.9 4.8 %copy-start = (bf16[1,432,5120]{2,1,0:T(8,128)(2,1)S(1)}, bf16[1,432,5120]{2,1,0:T(8,128)(2,1)}, u32[]{:S(2)}) copy-start(bf16[1,432,5120]{2,1,0:T(8,128)(2,1)} %get-tuple-element.112) | copy-start | bytes 13271044

commit v4 on v3

--- a/solution.py
+++ b/solution.py
@@ -519,13 +519,17 @@
         moment_store(k).wait()
     if relays:
 
-        @pl.when(lands | wraps)
-        def _():
-            def passed(j, carry):
-                pass_on_copy(j, x_beside).wait_send()
-                return carry
-
+        def passed(j, carry):
+            pass_on_copy(j, x_beside).wait_send()
+            return carry
+
+        @pl.when(lands)
+        def _():
             lax.fori_loop(0, relays, passed, 0)
+
+        @pl.when(wraps)
+        def _():
+            lax.fori_loop(relays, chunks, passed, 0)
 
     hidden_grad_store.wait()
 
@@ -535,7 +539,7 @@
     _, rows, depth = weight.shape
     chunks = depth // CHUNK
     unit = micro * tokens
-    relays = chunks // 2
+    relays = chunks * 15 // 20
     half = jnp.bfloat16
     anywhere = pl.BlockSpec(memory_space=pl.ANY)
     scratch = [

time: 172 us -> 171 us (level)
  the two profiles are of different devices: /device:TPU:113 before, /device:TPU:0 now
where the time goes in v4:
time: 171 us; the launch traced here: 170 us
  Pallas kernels  160 us (94%)
  local copies, waits for them, and re-layouts  8.08 us (5%)
    pallas_call x1, Pallas kernels, step_call(): pl.pallas_call(functools.partial(step_kernel, 1 << level, factor), out_sh...  160 us
    unnamed x5, local copies, waits for them, and re-layouts  8.08 us

profile of v4, /device:TPU:0, one launch (start us, length us, event | category | flops | bytes accessed | tf_op | source)
XLA Modules:
  0.0 170.2 jit_solution(5758710677531272175)
XLA Ops:
  1.4 0.1 pad_maximum_fusion
  1.5 160.7 %conditional.1 = ((bf16[1,432,5120]{2,1,0:T(8,128)(2,1)}, bf16[1,432,5120]{2,1,0:T(8,128)(2,1)}, bf16[1,2,64,6912]{3,2,1,0:T(8,128)(2,1)S(1)})) conditional(s32[]{:T(128)} %clamp.3, (f32[2]{0:T(128)S(1)}, bf16[1,2,64,6912]{3,2,1,0:T(8,128)(2,1)}, bf16[1,2,64,5120]{3,2,1,0:T(8,128)(2,1)}, bf16[1,432,5120]{2,1,0:T(8,128)(2,1)}, ...), branch_computations={%region_0.1_spmd, %region_1.2_spmd, %region_2.3_spmd} | conditional | flops 18119393280 | bytes 26968072 | solution.py:606
  1.5 160.4 %step_1.1 = (bf16[1,432,5120]{2,1,0:T(8,128)(2,1)}, bf16[1,432,5120]{2,1,0:T(8,128)(2,1)}, bf16[1,2,64,6912]{3,2,1,0:T(8,128)(2,1)S(1)}) custom-call(f32[2]{0:T(128)S(1)} %get-tuple-element.36.scale_ref, bf16[1,2,64,6912]{3,2,1,0:T(8,128)(2,1)} %get-tuple-element.84.hidden_hbm, bf16[1,2,64,5120]{3,2,1,0:T(8,128)(2,1)} %get-tuple-element.87.grads_hbm, ...), custom_call_target="tpu_custom_call" | custom-call | flops 18119393280 | bytes 26968064 | tf_op jit(solution)/shard_map/cond/branch_0_fun/step_1/pallas_call | solution.py:578
  162.1 0.0 copy-start
  162.1 4.8 %copy.46 = bf16[1,432,5120]{2,1,0:T(8,128)(2,1)} copy(bf16[1,432,5120]{2,1,0:T(8,128)(2,1)} %get-tuple-element.111) | data formatting | bytes 8847360
  166.9 0.0 copy-done
  166.9 2.1 %copy.47 = bf16[1,432,5120]{2,1,0:T(8,128)(2,1)} copy(bf16[1,432,5120]{2,1,0:T(8,128)(2,1)S(1)} %copy-done) | data formatting | bytes 8847360
  169.0 1.2 copy.48
Async XLA Ops:
  162.1 4.8 %copy-start = (bf16[1,432,5120]{2,1,0:T(8,128)(2,1)S(1)}, bf16[1,432,5120]{2,1,0:T(8,128)(2,1)}, u32[]{:S(2)}) copy-start(bf16[1,432,5120]{2,1,0:T(8,128)(2,1)} %get-tuple-element.112) | copy-start | bytes 13271044
